TPU v7x, 32 devices: a whole 2x2x4 slice. The times are simulated.
32 devices in a mesh: layer: 4 (over y, x), slab: 8 (over z, core).
Axes of the slice: x: 2, y: 2, z: 4, core: 2. Of those that a mesh axis runs over, the one named last changes fastest.
Arguments:
- activations: bfloat16 [4, 256, 8192], P(None, ('layer', 'slab')), may hold values from -6 to 6
- gram_prior: float32 [4, 8192, 8192], P('layer', None, 'slab'), as said below
- targets: float32 [4, 8192, 128], P('layer', 'slab'), may hold values from -6 to 6
- ridge: float32 [4], P('layer'), may hold values from 0.5 to 2
Outputs:
- gram_new: float32 [4, 8192, 8192], P('layer', None, 'slab')
- probe_weights: float32 [4, 8192, 128], P('layer', 'slab')
- residual: float32 [4, 8192, 128], P('layer', 'slab')
Inputs may be any that keep to these rules, and one draw needn't show every extreme that they name: `gram_prior`: each layer's matrix is exactly symmetric.
All inputs are finite; a program needn't handle non-finite values.
Results may differ from a plain program's by a relative error of at most 0.0003.
Values may be sent and summed in bfloat16 or wider, within the bound.
A program may use at most 256 MiB of HBM per device.

v0:
```python
import jax
import jax.numpy as jnp
from jax import lax
from jax.sharding import PartitionSpec as P

ITERS = 2


def squares(resid):
    return lax.psum(jnp.sum(resid * resid, axis=0), "slab")


def on_device(activations, gram_prior, targets, ridge):
    local_rows = lax.all_to_all(activations, "layer", split_axis=0, concat_axis=1, tiled=True)[0]
    width = gram_prior.shape[2]
    col_start = lax.axis_index("slab") * width
    total_tokens = local_rows.shape[0] * lax.axis_size("slab")
    gathered = lax.all_gather(local_rows, "slab", axis=0, tiled=True)
    own_cols = lax.dynamic_slice_in_dim(gathered, col_start, width, 1)
    gram = gram_prior[0] + lax.dot_general(
        gathered, own_cols, (((0,), (0,)), ((), ())), preferred_element_type=jnp.float32
    )
    lam = ridge[0]
    rhs = targets[0]
    weights = jnp.zeros_like(rhs)
    resid = rhs
    direction = rhs
    norm_now = squares(resid)
    for step in range(ITERS):
        vecs = direction
        mixed = lax.psum_scatter(
            jnp.dot(
                gram, vecs, precision=lax.Precision.HIGHEST, preferred_element_type=jnp.float32
            ),
            "slab",
            scatter_dimension=0,
            tiled=True,
        )
        image = mixed / total_tokens + lam * vecs
        alpha = norm_now / lax.psum(jnp.sum(direction * image, axis=0), "slab")
        weights = weights + alpha * direction
        resid = resid - alpha * image
        norm_next = squares(resid)
        direction = resid + norm_next / norm_now * direction
        norm_now = norm_next
    return (gram[None], weights[None], resid[None])


def solution(mesh):
    return jax.shard_map(
        on_device,
        mesh=mesh,
        in_specs=(
            P(None, ("layer", "slab"), None),
            P("layer", None, "slab"),
            P("layer", "slab", None),
            P("layer"),
        ),
        out_specs=(P("layer", None, "slab"), P("layer", "slab", None), P("layer", "slab", None)),
        check_vma=False,
    )
```

profile of v0, /device:TPU:0, one launch (start us, length us, event | category | flops | bytes accessed | tf_op | source)
XLA Modules:
  0.0 359.9 jit_solution(2196415275334460408)
XLA Ops:
  7.2 0.0 all-gather.2.cloned.1.call-start
  7.2 14.3 %all_to_all.4 = bf16[4,8,8192]{2,1,0:T(8,128)(2,1)} all-to-all(bf16[4,8,8192]{2,1,0:T(8,128)(2,1)} %param.4), channel_id=1, replica_groups=mesh['layer'=4,'slab'=8] {'layer'}, dimensions={0} | all-to-all | bytes 1048576 | tf_op jit(solution)/shard_map/all_to_all | solution.py:14
  21.5 0.0 all-gather.2.cloned.1.call-update
  21.5 0.0 reduce-scatter.3.cloned.1.call-start
  21.6 31.3 %copy.7 = f32[1,8192,1024]{1,2,0:T(8,128)} copy(f32[1,8192,1024]{2,1,0:T(8,128)} %param.5) | data formatting | bytes 67108864 | tf_op args[1]
  52.8 0.0 copy-start
  52.8 15.9 %all-gather.2.cloned.1.call-done = bf16[256,8192]{1,0:T(8,128)(2,1)} async-done(((bf16[32,8192]{1,0:T(8,128)(2,1)}), bf16[256,8192]{1,0:T(8,128)(2,1)}) %all-gather.2.cloned.1.call-update) | async-done | bytes 4194320 | tf_op jit(solution)/shard_map/all_gather | solution.py:18
  68.7 25.8 %bitcast_add_fusion = f32[8192,1024]{0,1:T(8,128)} fusion(f32[1,8192,1024]{1,2,0:T(8,128)} %copy.7, bf16[256,8192]{1,0:T(8,128)(2,1)} %all-gather.2.cloned.1.call-done, s32[]{:T(128)S(6)} %select_n.3), kind=kOutput, calls=%fused_computation | convolution fusion | flops 4303355904 | bytes 71827456 | tf_op jit(solution)/shard_map/dot_general | solution.py:20
  94.5 0.0 copy-done
  94.5 57.3 %fusion = f32[8192,128]{1,0:T(8,128)} fusion(f32[8192,1024]{0,1:T(8,128)} %bitcast_add_fusion, f32[1,1024,128]{2,1,0:T(8,128)S(1)} %copy-done), kind=kOutput, calls=%fused_computation.6 | convolution fusion | flops 12884901888 | bytes 38273024 | tf_op jit(solution)/shard_map/dot_general | solution.py:32
  151.8 0.0 reduce-scatter.3.cloned.1.call-update
  151.8 0.0 reduce-scatter.5.cloned.1.call-start
  152.5 48.2 %reduce-scatter.3.cloned.1.call-done = f32[1024,128]{1,0:T(8,128)} async-done(((f32[8192,128]{1,0:T(8,128)}), f32[1024,128]{1,0:T(8,128)}) %reduce-scatter.3.cloned.1.call-update) | async-done | bytes 524304 | tf_op jit(solution)/shard_map/reduce_scatter | solution.py:31
  200.7 1.2 fusion.4
  201.9 13.7 %all-reduce = (f32[128]{0:T(128)S(1)}, f32[128]{0:T(128)S(1)}) all-reduce(f32[128]{0:T(128)S(1)} %get-tuple-element.7, f32[128]{0:T(128)S(1)} %get-tuple-element.6), channel_id=1, replica_groups=mesh['layer'=4,'slab'=8] {'slab'}, use_global_device_ids=true, to_apply=%region_1.0 | all-reduce | flops 256 | bytes 2048 | tf_op jit(solution)/shard_map/psum | solution.py:10
  215.7 1.2 multiply_reduce_fusion.1
  216.9 13.6 %psum.30 = f32[128]{0:T(128)S(1)} all-reduce(f32[128]{0:T(128)S(1)} %multiply_reduce_fusion.1), channel_id=1, replica_groups=mesh['layer'=4,'slab'=8] {'slab'}, use_global_device_ids=true, to_apply=%region_6.0 | all-reduce | flops 128 | bytes 1024 | tf_op jit(solution)/shard_map/psum | solution.py:10
  230.5 57.2 %fusion.9 = f32[8192,128]{1,0:T(8,128)} fusion(f32[8192,1024]{0,1:T(8,128)} %bitcast_add_fusion, f32[1,1024,128]{2,1,0:T(8,128)S(1)} %copy-done, f32[128]{0:T(128)S(1)} %div.17, f32[1024,128]{1,0:T(8,128)} %reduce-scatter.3.cloned.1.call-done, f32[128]{0:T(128)S(1)} %div.16, f32[]{:T(128)} %bitcast.61), kind=kOutput, calls=%fused_computation.20 | convolution fusion | flops 12885819392 | bytes 38798340 | tf_op jit(solution)/shard_map/dot_general | solution.py:32
  287.7 0.0 reduce-scatter.5.cloned.1.call-update
  287.7 0.0 copy-start.1
  287.7 33.7 %copy.8 = f32[1,8192,1024]{2,1,0:T(8,128)} copy(f32[1,8192,1024]{1,2,0:T(8,128)} %bitcast.62) | data formatting | bytes 67108864
  321.4 14.6 %reduce-scatter.5.cloned.1.call-done = f32[1024,128]{1,0:T(8,128)} async-done(((f32[8192,128]{1,0:T(8,128)}), f32[1024,128]{1,0:T(8,128)}) %reduce-scatter.5.cloned.1.call-update) | async-done | bytes 524304 | tf_op jit(solution)/shard_map/reduce_scatter | solution.py:31
  336.0 0.0 copy-done.1
  336.0 1.3 multiply_reduce_fusion
  337.3 13.8 %psum.31 = f32[128]{0:T(128)S(1)} all-reduce(f32[128]{0:T(128)S(1)} %multiply_reduce_fusion), channel_id=1, replica_groups=mesh['layer'=4,'slab'=8] {'slab'}, use_global_device_ids=true, to_apply=%region_9.0 | all-reduce | flops 128 | bytes 1024 | tf_op jit(solution)/shard_map/psum | solution.py:40
  351.1 2.3 subtract_bitcast_fusion
  (3 shorter events, 0.0 us)
Async XLA Ops:
  7.2 61.5 %all-gather.2.cloned.1.call-start = ((), (), s32[]{:S(2)}) async-start(), calls=%async_computation.3 | async-start | bytes 4718592 | tf_op jit(solution)/shard_map/all_gather | solution.py:18
  21.5 179.2 %reduce-scatter.3.cloned.1.call-start = ((), (), s32[]{:S(2)}) async-start(), calls=%async_computation.4 | async-start | bytes 4718592 | tf_op jit(solution)/shard_map/reduce_scatter | solution.py:31
  52.8 41.7 %copy-start = (f32[1,1024,128]{2,1,0:T(8,128)S(1)}, f32[1,1024,128]{2,1,0:T(8,128)}, u32[]{:S(2)}) copy-start(f32[1,1024,128]{2,1,0:T(8,128)} %param.6) | copy-start | bytes 1572868
  151.8 184.2 %reduce-scatter.5.cloned.1.call-start = ((), (), s32[]{:S(2)}) async-start(), calls=%async_computation.5 | async-start | bytes 4718592 | tf_op jit(solution)/shard_map/reduce_scatter | solution.py:31
  287.7 48.3 %copy-start.1 = (f32[1024,128]{1,0:T(8,128)S(1)}, f32[1024,128]{1,0:T(8,128)}, u32[]{:S(2)}) copy-start(f32[1024,128]{1,0:T(8,128)} %reduce-scatter.3.cloned.1.call-done) | copy-start | bytes 1572868
Sparse Core Ops, SparseCore 0:
  21.6 47.0 all-gather.1
  151.9 48.7 reduce-scatter.2
  287.8 48.1 reduce-scatter.4
where the time goes:
time: 361 us; the launch traced here: 360 us
  matrix products  140 us (39%)
  waiting for transfers between devices  78.7 us (22%)
  local copies, waits for them, and re-layouts  65 us (18%)
  blocking collectives  55.4 us (15%)
  between operations  14.4 us (4%)
  other arithmetic  5.95 us (2%)
    dot_general x2, matrix products, on_device(): jnp.dot(gram, vecs, precision=lax.Precision.HIGHEST, preferred_element_ty...  115 us
    unnamed x6, local copies, waits for them, and re-layouts  65 us
    reduce_scatter x2, waiting for transfers between devices, on_device(): lax.psum_scatter(jnp.dot(gram, vecs, precision=lax.Precision.HIGHEST, pre...  62.8 us
    psum x2, blocking collectives, squares(): return lax.psum(jnp.sum(resid * resid, axis=0), 'slab')  27.3 us
    dot_general x1, matrix products, on_device(): lax.dot_general(gathered, own_cols, (((0,), (0,)), ((), ())), preferred_e...  25.8 us
    all_gather x1, waiting for transfers between devices, on_device(): gathered = lax.all_gather(local_rows, 'slab', axis=0, tiled=True)  15.9 us
    all_to_all x1, blocking collectives, on_device(): lax.all_to_all(activations, 'layer', split_axis=0, concat_axis=1, tiled=T...  14.3 us
    psum x1, blocking collectives, on_device(): alpha = norm_now / lax.psum(jnp.sum(direction * image, axis=0), 'slab')  13.8 us
  transfers between devices with their start and end apart: 3, of which 3 were waited for; matrix products, arithmetic and copies ran while one was open for 18% of the time, Pallas kernels for 0%

commit v1 on v0

v1 whole, which is shorter than its diff:
```python
import functools
import jax
import jax.numpy as jnp
from jax import lax
from jax.experimental import pallas as pl
from jax.experimental.pallas import tpu as pltpu
from jax.sharding import PartitionSpec as P

MESH = pl.DeviceIdType.MESH
F32 = jnp.float32
BF16 = jnp.bfloat16


def split(x):
    hi = x.astype(BF16)
    return hi, (x - hi.astype(F32)).astype(BF16)


def dot(a, b, dims=((1,), (0,))):
    return lax.dot_general(a, b, (dims, ((), ())), preferred_element_type=F32)


class Gather:
    def __init__(self, buf, sems, layer, slab, chips):
        self.buf, self.layer, self.chips = buf, layer, chips
        self.chip, self.core = slab // 2, slab % 2
        self.direct_send, self.direct_recv, self.pair_send, self.pair_recv = sems

    def slot(self, offset, core):
        return lax.rem(self.chip - offset + self.chips, self.chips) * 2 + core

    def direct(self, offset):
        mine = self.slot(0, self.core)
        there = lax.rem(self.chip + offset, self.chips) * 2 + self.core
        return pltpu.make_async_remote_copy(
            src_ref=self.buf.at[mine], dst_ref=self.buf.at[mine],
            send_sem=self.direct_send.at[offset], recv_sem=self.direct_recv.at[offset],
            device_id=(self.layer, there), device_id_type=MESH)

    def arrival(self, offset):
        here = self.slot(offset, self.core)
        return pltpu.make_async_remote_copy(
            src_ref=self.buf.at[here], dst_ref=self.buf.at[here],
            send_sem=self.direct_send.at[offset], recv_sem=self.direct_recv.at[offset],
            device_id=(self.layer, self.slot(0, 1 - self.core)), device_id_type=MESH)

    def pair(self, offset, core):
        here = self.slot(offset, core)
        return pltpu.make_async_remote_copy(
            src_ref=self.buf.at[here], dst_ref=self.buf.at[here],
            send_sem=self.pair_send.at[offset], recv_sem=self.pair_recv.at[offset],
            device_id=(self.layer, self.slot(0, 1 - self.core)), device_id_type=MESH)

    def order(self):
        out = []
        for k in range(1, self.chips // 2 + 1):
            out += sorted({k, self.chips - k})
        return out

    def start(self):
        for offset in self.order():
            self.direct(offset).start()
        self.pair(0, self.core).start()

    def take(self, offset):
        self.arrival(offset).wait_recv()
        self.pair(offset, self.core).start()

    def take_pair(self, offset):
        self.pair(offset, 1 - self.core).wait_recv()

    def finish(self):
        for offset in range(1, self.chips):
            self.direct(offset).wait_send()
        for offset in range(self.chips):
            self.pair(offset, self.core).wait_send()


def first_kernel(layers, slabs, act_ref, prior_ref, tgt_ref, ridge_ref,
                 x_out, xown_out, dir_out, d1_ref, r1_ref, w1_ref, rr_ref,
                 xs, xflat, r0, img, pbuf, acc, rrs, prior_sem, own_sem, lay_send, lay_recv, out_sem,
                 *sems):
    chips = slabs // 2
    width = tgt_ref.shape[1]
    layer, slab = lax.axis_index("layer"), lax.axis_index("slab")
    chip, core = slab // 2, slab % 2
    rows = act_ref.shape[1]
    tokens = layers * slabs * rows
    lam = ridge_ref[0]
    gx = Gather(xs, sems[0:4], layer, slab, chips)
    gr = Gather(r0, sems[4:8], layer, slab, chips)
    gi = Gather(img, sems[8:12], layer, slab, chips)

    order = [(0, 0), (0, 1)]
    for offset in gr.order():
        order += [(offset, 0), (offset, 1)]

    def slot_of(step):
        offset, other = order[step]
        return gr.slot(offset, 1 - core if other else core)

    def prior_copy(step):
        at = pl.multiple_of(slot_of(step) * width, width)
        return pltpu.make_async_copy(prior_ref.at[0, pl.ds(at, width), :], pbuf.at[step % 2], prior_sem.at[step % 2])

    prior_copy(0).start()
    own = pltpu.make_async_copy(act_ref.at[layer], xs.at[slab, layer], own_sem)
    own.start()
    r0[slab] = tgt_ref[0].T

    barrier = pltpu.get_barrier_semaphore()
    partners = [(lax.rem(layer + k, layers), slab) for k in range(1, layers)]
    partners += [(layer, lax.rem(chip + k, chips) * 2 + core) for k in range(1, chips)]
    partners += [(layer, chip * 2 + 1 - core)]
    for partner in partners:
        pl.semaphore_signal(barrier, inc=1, device_id=partner, device_id_type=MESH)
    pl.semaphore_wait(barrier, len(partners))

    def to_layer(k):
        there = lax.rem(layer + k, layers)
        return pltpu.make_async_remote_copy(
            src_ref=act_ref.at[there], dst_ref=xs.at[slab, layer],
            send_sem=lay_send.at[k], recv_sem=lay_recv.at[k],
            device_id=(there, slab), device_id_type=MESH)

    def from_layer(k):
        there = lax.rem(layer - k + layers, layers)
        return pltpu.make_async_remote_copy(
            src_ref=act_ref.at[there], dst_ref=xs.at[slab, there],
            send_sem=lay_send.at[k], recv_sem=lay_recv.at[k],
            device_id=(there, slab), device_id_type=MESH)

    for k in range(1, layers):
        to_layer(k).start()
    gr.start()
    own.wait()
    for k in range(1, layers):
        from_layer(k).wait_recv()
    gx.start()

    acc[...] = jnp.zeros_like(acc)
    rrs[...] = jnp.zeros_like(rrs)
    depth = min(256, width)
    half = acc.shape[0] // 2

    for step in range(len(order)):
        offset, other = order[step]
        if step + 1 < len(order):
            prior_copy(step + 1).start()
        if other:
            gr.take_pair(offset)
        elif offset:
            gr.take(offset)
        at_slot = slot_of(step)
        prior_copy(step).wait()

        @pl.loop(0, width // depth)
        def _(i):
            at = pl.multiple_of(i * depth, depth)
            v = r0[at_slot, :, pl.ds(at, depth)]
            vhi, vlo = split(v)
            ghi, glo = split(pbuf[step % 2, pl.ds(at, depth), :])
            acc[...] += dot(jnp.concatenate([vhi, vlo], axis=0), ghi)
            acc[:half, :] += dot(vhi, glo)
            rrs[0] += jnp.sum(v * v, axis=1, keepdims=True)

    def flatten(at_slot):
        at = pl.multiple_of(at_slot * (layers * rows), layers * rows)
        block = xs[at_slot].astype(F32)
        xflat[pl.ds(at, layers * rows), :] = block.reshape(layers * rows, block.shape[2]).astype(BF16)

    flatten(slab)
    gx.take_pair(0)
    flatten(gx.slot(0, 1 - core))
    for offset in gx.order():
        gx.take(offset)
        flatten(gx.slot(offset, core))
        gx.take_pair(offset)
        flatten(gx.slot(offset, 1 - core))
    own_at = pl.multiple_of(slab * width, width)
    x_copy = pltpu.make_async_copy(xflat, x_out, out_sem.at[0])
    xown_copy = pltpu.make_async_copy(xflat.at[:, pl.ds(own_at, width)], xown_out, out_sem.at[1])
    x_copy.start()
    xown_copy.start()

    def project(k, total):
        at = pl.multiple_of(k * width, width)
        both = jnp.concatenate(split(r0[k]), axis=0)
        return total + dot(both, xflat[:, pl.ds(at, width)], ((1,), (1,)))

    mix = lax.fori_loop(0, slabs, project, jnp.zeros((2 * half, tokens), F32))
    shi, slo = split(mix[:half] + mix[half:])
    xown = xflat[:, pl.ds(own_at, width)]
    total = acc[:half, :] + acc[half:, :] + dot(shi, xown) + dot(slo, xown)
    img[slab] = total / tokens + lam * r0[slab]

    gi.start()
    rrs[1] = jnp.sum(r0[slab] * img[slab], axis=1, keepdims=True)

    def curve(at_slot):
        rrs[1] += jnp.sum(r0[at_slot] * img[at_slot], axis=1, keepdims=True)

    gi.take_pair(0)
    curve(gi.slot(0, 1 - core))
    for offset in gi.order():
        gi.take(offset)
        curve(gi.slot(offset, core))
        gi.take_pair(offset)
        curve(gi.slot(offset, 1 - core))
    gx.finish()
    gr.finish()
    gi.finish()
    for k in range(1, layers):
        to_layer(k).wait_send()

    alpha = rrs[0] / rrs[1]
    rrs[2] = jnp.zeros_like(rrs[2])

    @pl.loop(0, slabs)
    def _(k):
        now = r0[k] - alpha * img[k]
        img[k] = now
        rrs[2] += jnp.sum(now * now, axis=1, keepdims=True)

    beta = rrs[2] / rrs[0]

    @pl.loop(0, slabs)
    def _(k):
        hi, lo = split(img[k] + beta * r0[k])
        at = pl.multiple_of(k * width, width)
        dir_out[:half, pl.ds(at, width)] = hi
        dir_out[half:, pl.ds(at, width)] = lo

    r1_ref[...] = img[slab]
    d1_ref[...] = img[slab] + beta * r0[slab]
    w1_ref[...] = alpha * r0[slab]
    rr_ref[...] = rrs[2]
    x_copy.wait()
    xown_copy.wait()


def gram_kernel(prior_ref, x_ref, xown_ref, dir_ref, gram_ref, image_ref, acc):
    @pl.when(pl.program_id(0) == 0)
    def _():
        acc[...] = jnp.zeros_like(acc)

    half = acc.shape[0] // 2
    depth = 256

    @pl.loop(0, prior_ref.shape[1] // depth)
    def _(i):
        at = pl.multiple_of(i * depth, depth)
        block = prior_ref[0, pl.ds(at, depth), :] + dot(x_ref[:, pl.ds(at, depth)], xown_ref[...], ((0,), (0,)))
        gram_ref[0, pl.ds(at, depth), :] = block
        ghi, glo = split(block)
        acc[...] += dot(dir_ref[:, pl.ds(at, depth)], ghi)
        acc[:half, :] += dot(dir_ref[:half, pl.ds(at, depth)], glo)

    @pl.when(pl.program_id(0) == pl.num_programs(0) - 1)
    def _():
        image_ref[...] = acc[:half, :] + acc[half:, :]


def last_kernel(slabs, tokens, raw_ref, d1_ref, r1_ref, w1_ref, rr_ref, ridge_ref,
                w_ref, r_ref, parts, send_sem, recv_sem):
    layer, slab = lax.axis_index("layer"), lax.axis_index("slab")
    barrier = pltpu.get_barrier_semaphore()
    for k in range(1, slabs):
        pl.semaphore_signal(barrier, inc=1, device_id=(layer, lax.rem(slab + k, slabs)), device_id_type=MESH)
    d1 = d1_ref[...]
    image = raw_ref[...] / tokens + ridge_ref[0] * d1
    curve = jnp.sum(d1 * image, axis=1, keepdims=True)
    wide = jnp.broadcast_to(curve, (curve.shape[0], 128))
    parts[0] = wide.T[:8]
    pl.semaphore_wait(barrier, slabs - 1)

    def send(k):
        return pltpu.make_async_remote_copy(
            src_ref=parts.at[0], dst_ref=parts.at[k], send_sem=send_sem.at[k], recv_sem=recv_sem.at[k],
            device_id=(layer, lax.rem(slab + k, slabs)), device_id_type=MESH)

    for k in range(1, slabs):
        send(k).start()
    for k in range(1, slabs):
        send(k).wait()
    total = jnp.sum(parts[...], axis=0)[:1]
    total = jnp.broadcast_to(total, (128, total.shape[1])).T[:, :1]
    alpha = rr_ref[...] / total
    w_ref[0] = (w1_ref[...] + alpha * d1).T
    r_ref[0] = (r1_ref[...] - alpha * image).T


def on_device(layers, slabs, activations, gram_prior, targets, ridge):
    size, width = gram_prior.shape[1], gram_prior.shape[2]
    count = targets.shape[2]
    rows = activations.shape[1]
    chips = slabs // 2
    tokens = layers * slabs * rows
    vmem, anywhere, smem = (pl.BlockSpec(memory_space=m) for m in (pltpu.VMEM, pl.ANY, pltpu.SMEM))
    block = jax.ShapeDtypeStruct((count, width), F32)
    dma = pltpu.SemaphoreType.DMA
    limit = 60 * 1024 * 1024
    gather_sems = [dma((chips,))] * 4
    x, xown, direction, d1, r1, w1, rr = pl.pallas_call(
        functools.partial(first_kernel, layers, slabs),
        out_shape=(
            jax.ShapeDtypeStruct((tokens, size), BF16),
            jax.ShapeDtypeStruct((tokens, width), BF16),
            jax.ShapeDtypeStruct((2 * count, size), BF16),
            block, block, block,
            jax.ShapeDtypeStruct((count, 1), F32),
        ),
        in_specs=[anywhere, anywhere, vmem, smem],
        out_specs=(anywhere, anywhere, vmem, vmem, vmem, vmem, vmem),
        scratch_shapes=[
            pltpu.VMEM((slabs, layers, rows, size), BF16),
            pltpu.VMEM((tokens, size), BF16),
            pltpu.VMEM((slabs, count, width), F32),
            pltpu.VMEM((slabs, count, width), F32),
            pltpu.VMEM((2, width, width), F32),
            pltpu.VMEM((2 * count, width), F32),
            pltpu.VMEM((3, count, 1), F32),
            dma((2,)), dma, dma((layers,)), dma((layers,)), dma((2,)),
        ] + gather_sems * 3,
        compiler_params=pltpu.CompilerParams(
            collective_id=0, has_side_effects=True, vmem_limit_bytes=limit),
        name="gather_and_first_step",
    )(activations, gram_prior, targets, ridge)

    step = min(512, size)
    gram, raw = pl.pallas_call(
        gram_kernel,
        grid=(size // step,),
        out_shape=(jax.ShapeDtypeStruct((1, size, width), F32), block),
        in_specs=[
            pl.BlockSpec((1, step, width), lambda i: (0, i, 0)),
            pl.BlockSpec((tokens, step), lambda i: (0, i)),
            pl.BlockSpec((tokens, width), lambda i: (0, 0)),
            pl.BlockSpec((2 * count, step), lambda i: (0, i)),
        ],
        out_specs=(
            pl.BlockSpec((1, step, width), lambda i: (0, i, 0)),
            pl.BlockSpec((count, width), lambda i: (0, 0)),
        ),
        scratch_shapes=[pltpu.VMEM((2 * count, width), F32)],
        compiler_params=pltpu.CompilerParams(vmem_limit_bytes=limit),
        name="gram_and_second_image",
    )(gram_prior, x, xown, direction)

    out = jax.ShapeDtypeStruct((1, width, count), F32)
    weights, resid = pl.pallas_call(
        functools.partial(last_kernel, slabs, tokens),
        out_shape=(out, out),
        in_specs=[vmem, vmem, vmem, vmem, vmem, smem],
        out_specs=(vmem, vmem),
        scratch_shapes=[pltpu.VMEM((slabs, 8, count), F32), dma((slabs,)), dma((slabs,))],
        compiler_params=pltpu.CompilerParams(collective_id=1, has_side_effects=True),
        name="second_step",
    )(raw, d1, r1, w1, rr, ridge)
    return gram, weights, resid


def solution(mesh):
    return jax.shard_map(
        functools.partial(on_device, mesh.shape["layer"], mesh.shape["slab"]),
        mesh=mesh,
        in_specs=(
            P(None, ("layer", "slab"), None),
            P("layer", None, "slab"),
            P("layer", "slab", None),
            P("layer"),
        ),
        out_specs=(P("layer", None, "slab"), P("layer", "slab", None), P("layer", "slab", None)),
        check_vma=False,
    )
```

time: 361 us -> 202 us (0.56)
  Pallas kernels: 0 us -> 196 us
  matrix products: 140 us -> 0 us
  waiting for transfers between devices: 78.7 us -> 0 us
  local copies, waits for them, and re-layouts: 65 us -> 3.74 us
  blocking collectives: 55.4 us -> 0 us
  between operations: 14.4 us -> 1.29 us
  other arithmetic: 5.95 us -> 0 us
    pallas_call x0 -> x3, Pallas kernels: none -> 196 us  [the longest x1 151 us: on_device(): pl.pallas_call(functools.partial(first_kernel, layers, slabs), out_shape=...]
    dot_general x3 -> x0, matrix products: 140 us -> none  [the longest x2 115 us: on_device(): jnp.dot(gram, vecs, precision=lax.Precision.HIGHEST, preferred_element_ty...]
    reduce_scatter x2 -> x0, waiting for transfers between devices: 62.8 us -> none  [on_device(): lax.psum_scatter(jnp.dot(gram, vecs, precision=lax.Precision.HIGHEST, pre...]
    unnamed x6 -> x2, local copies, waits for them, and re-layouts: 65 us -> 3.74 us
    psum x3 -> x0, blocking collectives: 41.1 us -> none  [the longest x2 27.3 us: squares(): return lax.psum(jnp.sum(resid * resid, axis=0), 'slab')]
    all_gather x1 -> x0, waiting for transfers between devices: 15.9 us -> none  [on_device(): gathered = lax.all_gather(local_rows, 'slab', axis=0, tiled=True)]
    all_to_all x1 -> x0, blocking collectives: 14.3 us -> none  [on_device(): lax.all_to_all(activations, 'layer', split_axis=0, concat_axis=1, tiled=T...]
    reduce_sum x3 -> x0, other arithmetic: 3.66 us -> none  [the longest x2 2.46 us: on_device(): alpha = norm_now / lax.psum(jnp.sum(direction * image, axis=0), 'slab')]
  transfers between devices with their start and end apart: 3 -> 0, of which waited for: 3 -> 0; matrix products, arithmetic and copies ran while one was open for 18% -> 0% of each run, Pallas kernels for 0% -> 0%
where the time goes in v1:
time: 202 us; the launch traced here: 201 us
  Pallas kernels  196 us (97%)
  local copies, waits for them, and re-layouts  3.74 us (2%)
    pallas_call x1, Pallas kernels, on_device(): pl.pallas_call(functools.partial(first_kernel, layers, slabs), out_shape=...  151 us
    pallas_call x1, Pallas kernels, on_device(): pl.pallas_call(gram_kernel, grid=(size // step,), out_shape=(jax.ShapeDty...  36.6 us
    pallas_call x1, Pallas kernels, on_device(): pl.pallas_call(functools.partial(last_kernel, slabs, tokens), out_shape=(...  8.52 us

profile of v1, /device:TPU:0, one launch (start us, length us, event | category | flops | bytes accessed | tf_op | source)
XLA Modules:
  0.0 201.1 jit_solution(7674814999092609340)
XLA Ops:
  1.3 151.0 %gather_and_first_step.1 = (bf16[256,8192]{1,0:T(8,128)(2,1)}, bf16[256,1024]{1,0:T(8,128)(2,1)}, bf16[256,8192]{1,0:T(8,128)(2,1)}, f32[128,1024]{1,0:T(8,128)}...) custom-call(bf16[4,8,8192]{2,1,0:T(8,128)(2,1)} %act_ref.1, f32[1,8192,1024]{2,1,0:T(8,128)} %prior_ref.3, ...), custom_call_target="tpu_custom_call" | custom-call | tf_op jit(solution)/shard_map/gather_and_first_step/pallas_call | solution.py:304
  152.3 36.6 %gram_and_second_image.1 = (f32[1,8192,1024]{2,1,0:T(8,128)}, f32[128,1024]{1,0:T(8,128)}) custom-call(f32[1,8192,1024]{2,1,0:T(8,128)} %prior_ref.3, bf16[256,8192]{1,0:T(8,128)(2,1)} %get-tuple-element.14.x_ref, bf16[256,1024]{1,0:T(8,128)(2,1)} %get-tuple-element.15.xown_ref, bf16[256,8192]{1,0:T(8,128)(2,1)} %get-tuple-element.16.dir_ref), custom_call_target="tpu_custom_call" | custom-call | tf_op jit(solution)/shard_map/gram_and_second_image/pallas_call | solution.py:331
  188.9 8.5 %second_step.1 = (f32[1,1024,128]{2,1,0:T(8,128)}, f32[1,1024,128]{2,1,0:T(8,128)}) custom-call(f32[128,1024]{1,0:T(8,128)} %get-tuple-element.18.raw_ref, f32[128,1024]{1,0:T(8,128)} %get-tuple-element.19.d1_ref, f32[128,1024]{1,0:T(8,128)} %get-tuple-element.20.r1_ref, f32[128,1024]{1,0:T(8,128)} %get-tuple-element.21.w1_ref, ...), custom_call_target="tpu_custom_call" | custom-call | tf_op jit(solution)/shard_map/second_step/pallas_call | solution.py:351
  197.4 1.9 copy.10
  199.3 1.9 copy.11

commit v2 on v1

--- a/solution.py
+++ b/solution.py
@@ -77,8 +77,8 @@
 
 
 def first_kernel(layers, slabs, act_ref, prior_ref, tgt_ref, ridge_ref,
-                 x_out, xown_out, dir_out, d1_ref, r1_ref, w1_ref, rr_ref,
-                 xs, xflat, r0, img, pbuf, acc, rrs, prior_sem, own_sem, lay_send, lay_recv, out_sem,
+                 x_out, xown_out, r0_out, image_ref,
+                 xs, xflat, r0, pbuf, acc, prior_sem, own_sem, lay_send, lay_recv, out_sem,
                  *sems):
     chips = slabs // 2
     width = tgt_ref.shape[1]
@@ -89,7 +89,6 @@
     lam = ridge_ref[0]
     gx = Gather(xs, sems[0:4], layer, slab, chips)
     gr = Gather(r0, sems[4:8], layer, slab, chips)
-    gi = Gather(img, sems[8:12], layer, slab, chips)
 
     order = [(0, 0), (0, 1)]
     for offset in gr.order():
@@ -139,7 +138,6 @@
     gx.start()
 
     acc[...] = jnp.zeros_like(acc)
-    rrs[...] = jnp.zeros_like(rrs)
     depth = min(256, width)
     half = acc.shape[0] // 2
 
@@ -162,7 +160,9 @@
             ghi, glo = split(pbuf[step % 2, pl.ds(at, depth), :])
             acc[...] += dot(jnp.concatenate([vhi, vlo], axis=0), ghi)
             acc[:half, :] += dot(vhi, glo)
-            rrs[0] += jnp.sum(v * v, axis=1, keepdims=True)
+
+    r0_copy = pltpu.make_async_copy(r0, r0_out, out_sem.at[2])
+    r0_copy.start()
 
     def flatten(at_slot):
         at = pl.multiple_of(at_slot * (layers * rows), layers * rows)
@@ -192,86 +192,79 @@
     shi, slo = split(mix[:half] + mix[half:])
     xown = xflat[:, pl.ds(own_at, width)]
     total = acc[:half, :] + acc[half:, :] + dot(shi, xown) + dot(slo, xown)
-    img[slab] = total / tokens + lam * r0[slab]
-
-    gi.start()
-    rrs[1] = jnp.sum(r0[slab] * img[slab], axis=1, keepdims=True)
-
-    def curve(at_slot):
-        rrs[1] += jnp.sum(r0[at_slot] * img[at_slot], axis=1, keepdims=True)
-
-    gi.take_pair(0)
-    curve(gi.slot(0, 1 - core))
-    for offset in gi.order():
-        gi.take(offset)
-        curve(gi.slot(offset, core))
-        gi.take_pair(offset)
-        curve(gi.slot(offset, 1 - core))
+    image_ref[...] = total / tokens + lam * r0[slab]
     gx.finish()
     gr.finish()
-    gi.finish()
     for k in range(1, layers):
         to_layer(k).wait_send()
-
-    alpha = rrs[0] / rrs[1]
-    rrs[2] = jnp.zeros_like(rrs[2])
-
-    @pl.loop(0, slabs)
-    def _(k):
-        now = r0[k] - alpha * img[k]
-        img[k] = now
-        rrs[2] += jnp.sum(now * now, axis=1, keepdims=True)
-
-    beta = rrs[2] / rrs[0]
-
-    @pl.loop(0, slabs)
-    def _(k):
-        hi, lo = split(img[k] + beta * r0[k])
-        at = pl.multiple_of(k * width, width)
-        dir_out[:half, pl.ds(at, width)] = hi
-        dir_out[half:, pl.ds(at, width)] = lo
-
-    r1_ref[...] = img[slab]
-    d1_ref[...] = img[slab] + beta * r0[slab]
-    w1_ref[...] = alpha * r0[slab]
-    rr_ref[...] = rrs[2]
+    r0_copy.wait()
     x_copy.wait()
     xown_copy.wait()
 
 
-def gram_kernel(prior_ref, x_ref, xown_ref, dir_ref, gram_ref, image_ref, acc):
-    @pl.when(pl.program_id(0) == 0)
-    def _():
-        acc[...] = jnp.zeros_like(acc)
-
-    half = acc.shape[0] // 2
+def gram_kernel(prior_ref, x_ref, xown_ref, gram_ref):
     depth = 256
-
-    @pl.loop(0, prior_ref.shape[1] // depth)
-    def _(i):
-        at = pl.multiple_of(i * depth, depth)
-        block = prior_ref[0, pl.ds(at, depth), :] + dot(x_ref[:, pl.ds(at, depth)], xown_ref[...], ((0,), (0,)))
-        gram_ref[0, pl.ds(at, depth), :] = block
-        ghi, glo = split(block)
-        acc[...] += dot(dir_ref[:, pl.ds(at, depth)], ghi)
-        acc[:half, :] += dot(dir_ref[:half, pl.ds(at, depth)], glo)
-
-    @pl.when(pl.program_id(0) == pl.num_programs(0) - 1)
-    def _():
-        image_ref[...] = acc[:half, :] + acc[half:, :]
-
-
-def last_kernel(slabs, tokens, raw_ref, d1_ref, r1_ref, w1_ref, rr_ref, ridge_ref,
-                w_ref, r_ref, parts, send_sem, recv_sem):
+    for at in range(0, prior_ref.shape[1], depth):
+        gram_ref[0, at:at + depth, :] = prior_ref[0, at:at + depth, :] + dot(
+            x_ref[:, at:at + depth], xown_ref[...], ((0,), (0,)))
+
+
+def second_kernel(slabs, tokens, gram_ref, r0_ref, img_ref, ridge_ref,
+                  w_ref, r_ref, gbuf, acc, sums, parts, gram_sem, send_sem, recv_sem):
     layer, slab = lax.axis_index("layer"), lax.axis_index("slab")
+    half, width = r0_ref.shape[1:]
+
+    def gram_copy(k):
+        return pltpu.make_async_copy(
+            gram_ref.at[0, pl.ds(k * width, width), :], gbuf.at[k % 3], gram_sem.at[k % 3])
+
+    for k in range(min(2, slabs)):
+        gram_copy(k).start()
     barrier = pltpu.get_barrier_semaphore()
     for k in range(1, slabs):
         pl.semaphore_signal(barrier, inc=1, device_id=(layer, lax.rem(slab + k, slabs)), device_id_type=MESH)
-    d1 = d1_ref[...]
-    image = raw_ref[...] / tokens + ridge_ref[0] * d1
+
+    acc[...] = jnp.zeros_like(acc)
+    sums[...] = jnp.zeros_like(sums)
+
+    def lanes(x):
+        return functools.reduce(jnp.add, [x[:, at:at + 128] for at in range(0, width, 128)])
+
+    @pl.loop(0, slabs)
+    def _(k):
+        r0 = r0_ref[k]
+        sums[0] += lanes(r0 * r0)
+        sums[1] += lanes(r0 * img_ref[k])
+
+    norm0 = jnp.sum(sums[0], axis=1, keepdims=True)
+    alpha0 = norm0 / jnp.sum(sums[1], axis=1, keepdims=True)
+
+    @pl.loop(0, slabs)
+    def _(k):
+        r1 = r0_ref[k] - alpha0 * img_ref[k]
+        sums[2] += lanes(r1 * r1)
+
+    norm1 = jnp.sum(sums[2], axis=1, keepdims=True)
+    beta = norm1 / norm0
+    depth = min(256, width)
+
+    for k in range(slabs):
+        if k + 2 < slabs:
+            gram_copy(k + 2).start()
+        gram_copy(k).wait()
+        for at in range(0, width, depth):
+            r0 = r0_ref[k, :, at:at + depth]
+            vhi, vlo = split(r0 - alpha0 * img_ref[k, :, at:at + depth] + beta * r0)
+            ghi, glo = split(gbuf[k % 3, at:at + depth, :])
+            acc[...] += dot(jnp.concatenate([vhi, vlo], axis=0), ghi)
+            acc[:half, :] += dot(vhi, glo)
+
+    r0 = r0_ref[slab]
+    r1 = r0 - alpha0 * img_ref[slab]
+    d1 = r1 + beta * r0
+    image = (acc[:half, :] + acc[half:, :]) / tokens + ridge_ref[0] * d1
     curve = jnp.sum(d1 * image, axis=1, keepdims=True)
-    wide = jnp.broadcast_to(curve, (curve.shape[0], 128))
-    parts[0] = wide.T[:8]
+    parts[0] = jnp.broadcast_to(curve, (half, 128)).T[:8]
     pl.semaphore_wait(barrier, slabs - 1)
 
     def send(k):
@@ -284,10 +277,10 @@
     for k in range(1, slabs):
         send(k).wait()
     total = jnp.sum(parts[...], axis=0)[:1]
-    total = jnp.broadcast_to(total, (128, total.shape[1])).T[:, :1]
-    alpha = rr_ref[...] / total
-    w_ref[0] = (w1_ref[...] + alpha * d1).T
-    r_ref[0] = (r1_ref[...] - alpha * image).T
+    total = jnp.broadcast_to(total, (128, half)).T[:, :1]
+    alpha1 = norm1 / total
+    w_ref[0] = (alpha0 * r0 + alpha1 * d1).T
+    r_ref[0] = (r1 - alpha1 * image).T
 
 
 def on_device(layers, slabs, activations, gram_prior, targets, ridge):
@@ -300,63 +293,64 @@
     block = jax.ShapeDtypeStruct((count, width), F32)
     dma = pltpu.SemaphoreType.DMA
     limit = 60 * 1024 * 1024
-    gather_sems = [dma((chips,))] * 4
-    x, xown, direction, d1, r1, w1, rr = pl.pallas_call(
+    x, xown, r0, image = pl.pallas_call(
         functools.partial(first_kernel, layers, slabs),
         out_shape=(
             jax.ShapeDtypeStruct((tokens, size), BF16),
             jax.ShapeDtypeStruct((tokens, width), BF16),
-            jax.ShapeDtypeStruct((2 * count, size), BF16),
-            block, block, block,
-            jax.ShapeDtypeStruct((count, 1), F32),
+            jax.ShapeDtypeStruct((slabs, count, width), F32),
+            block,
         ),
         in_specs=[anywhere, anywhere, vmem, smem],
-        out_specs=(anywhere, anywhere, vmem, vmem, vmem, vmem, vmem),
+        out_specs=(anywhere, anywhere, anywhere, vmem),
         scratch_shapes=[
             pltpu.VMEM((slabs, layers, rows, size), BF16),
             pltpu.VMEM((tokens, size), BF16),
             pltpu.VMEM((slabs, count, width), F32),
-            pltpu.VMEM((slabs, count, width), F32),
             pltpu.VMEM((2, width, width), F32),
             pltpu.VMEM((2 * count, width), F32),
-            pltpu.VMEM((3, count, 1), F32),
-            dma((2,)), dma, dma((layers,)), dma((layers,)), dma((2,)),
-        ] + gather_sems * 3,
+            dma((2,)), dma, dma((layers,)), dma((layers,)), dma((3,)),
+        ] + [dma((chips,))] * 8,
         compiler_params=pltpu.CompilerParams(
             collective_id=0, has_side_effects=True, vmem_limit_bytes=limit),
-        name="gather_and_first_step",
+        name="gather_and_first_image",
     )(activations, gram_prior, targets, ridge)
+    images = lax.all_gather(image, "slab")
 
     step = min(512, size)
-    gram, raw = pl.pallas_call(
+    gram = pl.pallas_call(
         gram_kernel,
         grid=(size // step,),
-        out_shape=(jax.ShapeDtypeStruct((1, size, width), F32), block),
+        out_shape=jax.ShapeDtypeStruct((1, size, width), F32),
         in_specs=[
             pl.BlockSpec((1, step, width), lambda i: (0, i, 0)),
             pl.BlockSpec((tokens, step), lambda i: (0, i)),
             pl.BlockSpec((tokens, width), lambda i: (0, 0)),
-            pl.BlockSpec((2 * count, step), lambda i: (0, i)),
         ],
-        out_specs=(
-            pl.BlockSpec((1, step, width), lambda i: (0, i, 0)),
-            pl.BlockSpec((count, width), lambda i: (0, 0)),
-        ),
-        scratch_shapes=[pltpu.VMEM((2 * count, width), F32)],
+        out_specs=pl.BlockSpec((1, step, width), lambda i: (0, i, 0)),
+        cost_estimate=pl.CostEstimate(
+            flops=2 * size * width * tokens, bytes_accessed=8 * size * width, transcendentals=0),
         compiler_params=pltpu.CompilerParams(vmem_limit_bytes=limit),
-        name="gram_and_second_image",
-    )(gram_prior, x, xown, direction)
+        name="gram_update",
+    )(gram_prior, x, xown)
 
     out = jax.ShapeDtypeStruct((1, width, count), F32)
     weights, resid = pl.pallas_call(
-        functools.partial(last_kernel, slabs, tokens),
+        functools.partial(second_kernel, slabs, tokens),
         out_shape=(out, out),
-        in_specs=[vmem, vmem, vmem, vmem, vmem, smem],
+        in_specs=[anywhere, vmem, vmem, smem],
         out_specs=(vmem, vmem),
-        scratch_shapes=[pltpu.VMEM((slabs, 8, count), F32), dma((slabs,)), dma((slabs,))],
-        compiler_params=pltpu.CompilerParams(collective_id=1, has_side_effects=True),
-        name="second_step",
-    )(raw, d1, r1, w1, rr, ridge)
+        scratch_shapes=[
+            pltpu.VMEM((3, width, width), F32),
+            pltpu.VMEM((2 * count, width), F32),
+            pltpu.VMEM((3, count, 128), F32),
+            pltpu.VMEM((slabs, 8, count), F32),
+            dma((3,)), dma((slabs,)), dma((slabs,)),
+        ],
+        compiler_params=pltpu.CompilerParams(
+            collective_id=1, has_side_effects=True, vmem_limit_bytes=limit),
+        name="second_image_and_step",
+    )(gram, r0, images, ridge)
     return gram, weights, resid
 
 

time: 202 us -> 189 us (0.936)
  Pallas kernels: 196 us -> 153 us
  waiting for transfers between devices: 0 us -> 17.7 us
  between operations: 1.29 us -> 14.7 us
    pallas_call x1, Pallas kernels: 151 us -> 103 us  [on_device(): pl.pallas_call(functools.partial(first_kernel, layers, slabs), out_shape=...]
    all_gather x0 -> x1, waiting for transfers between devices: none -> 17.7 us  [on_device(): images = lax.all_gather(image, 'slab')]
    pallas_call x2, Pallas kernels: 45.1 us -> 49.8 us  [the longest x1 29.9 us: on_device(): pl.pallas_call(gram_kernel, grid=(size // step,), out_shape=jax.ShapeDtyp...]
  transfers between devices with their start and end apart: 0 -> 1, of which waited for: 0 -> 1; matrix products, arithmetic and copies ran while one was open for 0% -> 0% of each run, Pallas kernels for 0% -> 16%
where the time goes in v2:
time: 189 us
  Pallas kernels  153 us (81%)
  waiting for transfers between devices  17.7 us (9%)
  between operations  14.7 us (8%)
  local copies, waits for them, and re-layouts  3.74 us (2%)
    pallas_call x1, Pallas kernels, on_device(): pl.pallas_call(functools.partial(first_kernel, layers, slabs), out_shape=...  103 us
    pallas_call x1, Pallas kernels, on_device(): pl.pallas_call(gram_kernel, grid=(size // step,), out_shape=jax.ShapeDtyp...  29.9 us
    pallas_call x1, Pallas kernels, on_device(): pl.pallas_call(functools.partial(second_kernel, slabs, tokens), out_shape...  19.8 us
    all_gather x1, waiting for transfers between devices, on_device(): images = lax.all_gather(image, 'slab')  17.7 us
  transfers between devices with their start and end apart: 1, of which 1 were waited for; matrix products, arithmetic and copies ran while one was open for 0% of the time, Pallas kernels for 16%

profile of v2, /device:TPU:0, one launch (start us, length us, event | category | flops | bytes accessed | tf_op | source)
XLA Modules:
  0.0 188.8 jit_solution(17752507263565637594)
XLA Ops:
  7.2 0.0 all-gather.3.cloned.1.call-start
  7.9 102.9 %gather_and_first_image.1 = (bf16[256,8192]{1,0:T(8,128)(2,1)}, bf16[256,1024]{1,0:T(8,128)(2,1)}, f32[8,128,1024]{2,1,0:T(8,128)}, f32[128,1024]{1,0:T(8,128)}) custom-call(bf16[4,8,8192]{2,1,0:T(8,128)(2,1)} %act_ref.1, f32[1,8192,1024]{2,1,0:T(8,128)} %prior_ref.3, f32[1,1024,128]{2,1,0:T(8,128)} %tgt_ref.1, f32[1]{0:T(128)S(6)} %copy.9.ridge_ref), custom_call_target="tpu_custom_call" | custom-call | tf_op jit(solution)/shard_map/gather_and_first_image/pallas_call | solution.py:296
  110.7 0.0 all-gather.3.cloned.1.call-update
  110.8 29.9 %gram_update.1.gram_ref = f32[1,8192,1024]{2,1,0:T(8,128)} custom-call(f32[1,8192,1024]{2,1,0:T(8,128)} %prior_ref.3, bf16[256,8192]{1,0:T(8,128)(2,1)} %get-tuple-element.9.x_ref, bf16[256,1024]{1,0:T(8,128)(2,1)} %get-tuple-element.10.xown_ref), custom_call_target="tpu_custom_call" | custom-call | flops 4294967296 | bytes 67108864 | tf_op jit(solution)/shard_map/gram_update/pallas_call | solution.py:321
  140.7 17.7 %all-gather.3.cloned.1.call-done = f32[1024,1024]{1,0:T(8,128)} async-done(((f32[128,1024]{1,0:T(8,128)}), f32[1024,1024]{1,0:T(8,128)}) %all-gather.3.cloned.1.call-update) | async-done | bytes 4194320 | tf_op jit(solution)/shard_map/all_gather | solution.py:318
  158.4 19.8 %second_image_and_step.1 = (f32[1,1024,128]{2,1,0:T(8,128)}, f32[1,1024,128]{2,1,0:T(8,128)}) custom-call(f32[1,8192,1024]{2,1,0:T(8,128)} %gram_update.1.gram_ref, f32[8,128,1024]{2,1,0:T(8,128)} %get-tuple-element.11.r0_ref, f32[8,128,1024]{2,1,0:T(8,128)} %bitcast.1, f32[1]{0:T(128)S(6)} %copy.9.ridge_ref), custom_call_target="tpu_custom_call" | custom-call | tf_op jit(solution)/shard_map/second_image_and_step/pallas_call | solution.py:338
  178.2 1.9 copy.10
  180.1 1.9 copy.11
Async XLA Ops:
  7.2 151.2 %all-gather.3.cloned.1.call-start = ((), (), s32[]{:S(2)}) async-start(), calls=%async_computation | async-start | bytes 4718592 | tf_op jit(solution)/shard_map/all_gather | solution.py:318
Sparse Core Ops, SparseCore 0:
  110.9 47.4 all-gather.2

commit v3 on v2

--- a/solution.py
+++ b/solution.py
@@ -279,8 +279,8 @@
     total = jnp.sum(parts[...], axis=0)[:1]
     total = jnp.broadcast_to(total, (128, half)).T[:, :1]
     alpha1 = norm1 / total
-    w_ref[0] = (alpha0 * r0 + alpha1 * d1).T
-    r_ref[0] = (r1 - alpha1 * image).T
+    w_ref[...] = alpha0 * r0 + alpha1 * d1
+    r_ref[...] = r1 - alpha1 * image
 
 
 def on_device(layers, slabs, activations, gram_prior, targets, ridge):
@@ -334,10 +334,9 @@
         name="gram_update",
     )(gram_prior, x, xown)
 
-    out = jax.ShapeDtypeStruct((1, width, count), F32)
     weights, resid = pl.pallas_call(
         functools.partial(second_kernel, slabs, tokens),
-        out_shape=(out, out),
+        out_shape=(block, block),
         in_specs=[anywhere, vmem, vmem, smem],
         out_specs=(vmem, vmem),
         scratch_shapes=[
@@ -351,7 +350,7 @@
             collective_id=1, has_side_effects=True, vmem_limit_bytes=limit),
         name="second_image_and_step",
     )(gram, r0, images, ridge)
-    return gram, weights, resid
+    return gram, weights.T[None], resid.T[None]
 
 
 def solution(mesh):

time: 189 us -> 190 us (level)
  no operation moved by 1% of the time
where the time goes in v3:
time: 190 us; the launch traced here: 189 us
  Pallas kernels  153 us (81%)
  waiting for transfers between devices  17.7 us (9%)
  between operations  14.7 us (8%)
  local copies, waits for them, and re-layouts  4.07 us (2%)
    pallas_call x1, Pallas kernels, on_device(): pl.pallas_call(functools.partial(first_kernel, layers, slabs), out_shape=...  103 us
    pallas_call x1, Pallas kernels, on_device(): pl.pallas_call(gram_kernel, grid=(size // step,), out_shape=jax.ShapeDtyp...  29.9 us
    pallas_call x1, Pallas kernels, on_device(): pl.pallas_call(functools.partial(second_kernel, slabs, tokens), out_shape...  19.7 us
    all_gather x1, waiting for transfers between devices, on_device(): images = lax.all_gather(image, 'slab')  17.7 us
    unnamed x2, local copies, waits for them, and re-layouts  4.07 us
  transfers between devices with their start and end apart: 1, of which 1 were waited for; matrix products, arithmetic and copies ran while one was open for 0% of the time, Pallas kernels for 16%

profile of v3, /device:TPU:0, one launch (start us, length us, event | category | flops | bytes accessed | tf_op | source)
XLA Modules:
  0.0 189.1 jit_solution(15982927868999951529)
XLA Ops:
  7.2 0.0 all-gather.3.cloned.1.call-start
  7.9 102.9 %gather_and_first_image.1 = (bf16[256,8192]{1,0:T(8,128)(2,1)}, bf16[256,1024]{1,0:T(8,128)(2,1)}, f32[8,128,1024]{2,1,0:T(8,128)}, f32[128,1024]{1,0:T(8,128)}) custom-call(bf16[4,8,8192]{2,1,0:T(8,128)(2,1)} %act_ref.1, f32[1,8192,1024]{2,1,0:T(8,128)} %prior_ref.3, f32[1,1024,128]{2,1,0:T(8,128)} %tgt_ref.1, f32[1]{0:T(128)S(6)} %copy.9.ridge_ref), custom_call_target="tpu_custom_call" | custom-call | tf_op jit(solution)/shard_map/gather_and_first_image/pallas_call | solution.py:296
  110.7 0.0 all-gather.3.cloned.1.call-update
  110.8 29.9 %gram_update.1.gram_ref = f32[1,8192,1024]{2,1,0:T(8,128)} custom-call(f32[1,8192,1024]{2,1,0:T(8,128)} %prior_ref.3, bf16[256,8192]{1,0:T(8,128)(2,1)} %get-tuple-element.9.x_ref, bf16[256,1024]{1,0:T(8,128)(2,1)} %get-tuple-element.10.xown_ref), custom_call_target="tpu_custom_call" | custom-call | flops 4294967296 | bytes 67108864 | tf_op jit(solution)/shard_map/gram_update/pallas_call | solution.py:321
  140.7 17.7 %all-gather.3.cloned.1.call-done = f32[1024,1024]{1,0:T(8,128)} async-done(((f32[128,1024]{1,0:T(8,128)}), f32[1024,1024]{1,0:T(8,128)}) %all-gather.3.cloned.1.call-update) | async-done | bytes 4194320 | tf_op jit(solution)/shard_map/all_gather | solution.py:318
  158.4 19.7 %second_image_and_step.1 = (f32[128,1024]{1,0:T(8,128)}, f32[128,1024]{1,0:T(8,128)}) custom-call(f32[1,8192,1024]{2,1,0:T(8,128)} %gram_update.1.gram_ref, f32[8,128,1024]{2,1,0:T(8,128)} %get-tuple-element.11.r0_ref, f32[8,128,1024]{2,1,0:T(8,128)} %bitcast.7, f32[1]{0:T(128)S(6)} %copy.9.ridge_ref), custom_call_target="tpu_custom_call" | custom-call | tf_op jit(solution)/shard_map/second_image_and_step/pallas_call | solution.py:337
  178.1 2.0 %copy.7 = f32[1,1024,128]{2,1,0:T(8,128)} copy(f32[1,1024,128]{1,2,0:T(8,128)} %bitcast.9) | data formatting | bytes 1048576
  180.2 2.0 %copy.8 = f32[1,1024,128]{2,1,0:T(8,128)} copy(f32[1,1024,128]{1,2,0:T(8,128)} %bitcast.8) | data formatting | bytes 1048576
Async XLA Ops:
  7.2 151.2 %all-gather.3.cloned.1.call-start = ((), (), s32[]{:S(2)}) async-start(), calls=%async_computation | async-start | bytes 4718592 | tf_op jit(solution)/shard_map/all_gather | solution.py:318
Sparse Core Ops, SparseCore 0:
  110.9 47.4 all-gather.2
